TPU v7x, 512 devices: a whole 4x4x16 slice. The times are simulated.
512 devices in a mesh: expert: 32 (over z, core), hidden: 16 (over x, y).
Axes of the slice: x: 4, y: 4, z: 16, core: 2. Of those that a mesh axis runs over, the one named last changes fastest.
Arguments:
- tokens: bfloat16 [16384, 768], P('expert', 'hidden'), may hold values from -6 to 6
- routes: int32 [16384, 1], P('expert'), may hold values from 0 to 127; in each aligned block of 512 rows (0 to 511, 512 to 1023, ...) at most 8 rows name the same one
- gate_value: float32 [16384, 1], P('expert'), may hold values from 0.2 to 1
- weight_in: bfloat16 [128, 768, 3072], P('expert', None, 'hidden'), may hold values from -0.21875 to 0.21875
- weight_out: bfloat16 [128, 3072, 768], P('expert', 'hidden'), may hold values from -0.109375 to 0.109375
- cotangent: bfloat16 [16384, 768], P('expert', 'hidden'), may hold values from -6 to 6
Outputs:
- layer_out: bfloat16 [16384, 768], P('expert', 'hidden')
- grad_tokens: bfloat16 [16384, 768], P('expert', 'hidden')
- grad_weight_in: bfloat16 [128, 768, 3072], P('expert', None, 'hidden')
- grad_weight_out: bfloat16 [128, 3072, 768], P('expert', 'hidden')
Inputs may be any that keep to these rules, and one draw needn't show every extreme that they name: `routes`: within each group of 512 consecutive tokens (the tokens of one index of the expert axis) no expert is chosen by more than 8 tokens; in some group some expert is chosen by exactly 8. Every expert is chosen by some token.
All inputs are finite; a program needn't handle non-finite values.
Results may differ from a plain program's by a relative error of at most 0.019.
Values may be sent and summed in bfloat16 or wider, within the bound.
A program may use at most 64 MiB of HBM per device.

v0:
```python
import jax
import jax.numpy as jnp
from jax import lax
from jax.sharding import PartitionSpec as P


def gelu_tanh(values):
    return jax.nn.gelu(values, approximate=True)


def local_places(routes, experts, capacity):
    chosen = routes[:, 0]
    matches = (chosen[:, None] == jnp.arange(experts, dtype=jnp.int32)[None, :]).astype(jnp.int32)
    before = jnp.cumsum(matches, axis=0) - matches
    return chosen * capacity + jnp.sum(before * matches, axis=1)


def local(tokens, routes, gate_value, weight_in, weight_out, cotangent):
    owners = lax.axis_size("expert")
    blocks = lax.axis_size("hidden")
    exp_dev = weight_in.shape[0]
    experts = owners * exp_dev
    capacity = max(2, 2 * tokens.shape[0] // experts)
    slot_count = experts * capacity
    features = tokens.shape[1]
    full_width = weight_out.shape[2]
    units = weight_in.shape[2]
    line = exp_dev * capacity * features
    placed = local_places(routes, experts, capacity)
    scaled = (gate_value * cotangent.astype(jnp.float32)).astype(jnp.bfloat16)
    first_four = weight_in.reshape(exp_dev, blocks, features, units)
    second_four = weight_out.reshape(exp_dev, units, blocks, features)

    def to_slots(values):
        filled = jnp.zeros((slot_count, features), jnp.bfloat16).at[placed].set(values)
        return filled.reshape(owners, line)

    def by_expert(gathered):
        return gathered.reshape(blocks, owners, exp_dev, capacity, features)

    arrived = (
        lax.all_to_all(to_slots(tokens), "expert", split_axis=0, concat_axis=0, tiled=True),
        lax.all_to_all(to_slots(scaled), "expert", split_axis=0, concat_axis=0, tiled=True),
    )
    rows_x, rows_g = (
        lax.all_gather(arrived[0][None], "hidden", axis=0, tiled=True),
        lax.all_gather(arrived[1][None], "hidden", axis=0, tiled=True),
    )
    rows_x = by_expert(rows_x)
    rows_g = by_expert(rows_g)
    preact = jnp.einsum("nsecf,enfh->sech", rows_x, first_four, preferred_element_type=jnp.float32)
    activation, pullback = jax.vjp(gelu_tanh, preact)
    hidden_act = activation.astype(jnp.bfloat16)
    out_part = jnp.einsum(
        "sech,ehnf->nsecf", hidden_act, second_four, preferred_element_type=jnp.float32
    )
    grad_hidden = jnp.einsum(
        "nsecf,ehnf->sech", rows_g, second_four, preferred_element_type=jnp.float32
    )
    grad_pre = pullback(grad_hidden)[0].astype(jnp.bfloat16)
    grad_part = jnp.einsum(
        "sech,enfh->nsecf", grad_pre, first_four, preferred_element_type=jnp.float32
    )
    grad_weight_in = (
        jnp.einsum("nsecf,sech->enfh", rows_x, grad_pre, preferred_element_type=jnp.float32)
        .astype(jnp.bfloat16)
        .reshape(exp_dev, full_width, units)
    )
    grad_weight_out = (
        jnp.einsum("sech,nsecf->ehnf", hidden_act, rows_g, preferred_element_type=jnp.float32)
        .astype(jnp.bfloat16)
        .reshape(exp_dev, units, full_width)
    )
    flat_out = out_part.reshape(blocks, owners, line)
    flat_grad = grad_part.reshape(blocks, owners, line)
    summed = (
        lax.psum_scatter(
            flat_out.astype(jnp.bfloat16), "hidden", scatter_dimension=0, tiled=True
        ).astype(jnp.float32),
        lax.psum_scatter(
            flat_grad.astype(jnp.bfloat16), "hidden", scatter_dimension=0, tiled=True
        ).astype(jnp.float32),
    )
    out_rows = summed[0][0].astype(jnp.bfloat16)
    grad_rows = summed[1][0].astype(jnp.bfloat16)
    back_out, back_grad = (
        lax.all_to_all(out_rows, "expert", split_axis=0, concat_axis=0, tiled=True),
        lax.all_to_all(grad_rows, "expert", split_axis=0, concat_axis=0, tiled=True),
    )
    layer_out = (
        gate_value * back_out.reshape(slot_count, features)[placed].astype(jnp.float32)
    ).astype(jnp.bfloat16)
    grad_tokens = back_grad.reshape(slot_count, features)[placed]
    return (layer_out, grad_tokens, grad_weight_in, grad_weight_out)


def solution(mesh):
    in_specs = (
        P("expert", "hidden"),
        P("expert", None),
        P("expert", None),
        P("expert", None, "hidden"),
        P("expert", "hidden", None),
        P("expert", "hidden"),
    )
    out_specs = (
        P("expert", "hidden"),
        P("expert", "hidden"),
        P("expert", None, "hidden"),
        P("expert", "hidden", None),
    )
    return jax.shard_map(local, mesh=mesh, in_specs=in_specs, out_specs=out_specs, check_vma=False)
```

profile of v0, /device:TPU:1, one launch (start us, length us, event | category | flops | bytes accessed | tf_op | source)
XLA Modules:
  0.0 383.4 jit_solution(2503583013472697670)
XLA Ops:
  7.2 0.0 all-gather.5.cloned.1.call-start
  7.2 0.8 copy.66
  8.0 0.9 copy.68
  8.9 0.2 fusion.29
  9.3 0.2 fusion.28
  9.6 1.8 scatter_custom_fusion
  11.4 0.3 all_to_all.26
  11.7 0.5 broadcast.93
  12.2 1.2 reduce.2
  13.5 31.3 %all_to_all.32 = bf16[32,2,768]{2,1,0:T(2,128)(2,1)S(1)} all-to-all(bf16[32,2,768]{2,1,0:T(2,128)(2,1)S(1)} %reshape.156), channel_id=1, replica_groups=mesh['expert'=32,'hidden'=16] {'expert'}, dimensions={0} | all-to-all | bytes 196608 | tf_op jit(solution)/shard_map/all_to_all | solution.py:42
  44.8 0.1 reshape.157
  44.9 0.7 copy.70
  45.5 0.0 all-gather.7.cloned.1.call-start
  45.6 0.1 copy.77
  45.7 1.9 scatter_custom_fusion.1
  47.7 0.3 all_to_all.27
  48.0 1.2 reduce.4
  49.2 18.2 %all_to_all.33 = bf16[32,2,768]{2,1,0:T(2,128)(2,1)S(1)} all-to-all(bf16[32,2,768]{2,1,0:T(2,128)(2,1)S(1)} %reshape.160), channel_id=1, replica_groups=mesh['expert'=32,'hidden'=16] {'expert'}, dimensions={0} | all-to-all | bytes 196608 | tf_op jit(solution)/shard_map/all_to_all | solution.py:43
  67.4 0.1 reshape.161
  67.5 0.7 copy.79
  68.2 0.0 all-gather.7.cloned.1.call-update
  68.2 0.2 reduce-scatter.7.cloned.1.call-start
  68.4 0.7 copy.71
  69.1 1.6 copy.74
  70.7 25.1 %all-gather.5.cloned.1.call-done = bf16[512,1,1536]{2,0,1:T(8,128)(2,1)} async-done(((bf16[32,1,1536]{2,0,1:T(8,128)(2,1)}), bf16[512,1,1536]{2,0,1:T(8,128)(2,1)}) %all-gather.5.cloned.1.call-update) | async-done | bytes 1572880 | tf_op jit(solution)/shard_map/all_gather | solution.py:46
  95.8 6.8 %reshape.92 = bf16[16,32,4,8,48]{4,3,2,1,0:T(8,128)(2,1)} reshape(bf16[512,1,1536]{2,0,1:T(8,128)(2,1)} %all-gather.5.cloned.1.call-done) | data formatting | bytes 3145728 | tf_op jit(solution)/shard_map/reshape | solution.py:39
  102.6 3.4 fusion.10
  106.1 1.0 copy-done.1
  107.0 1.3 convert_bitcast_fusion.1
  108.3 3.1 copy.75
  111.4 8.7 %convert_element_type.78 = bf16[16,32,1536]{2,1,0:T(8,128)(2,1)} reshape(bf16[16,32,4,8,48]{4,3,2,1,0:T(8,128)(2,1)} %copy.75) | data formatting | bytes 3145728 | tf_op jit(solution)/shard_map/convert_element_type | solution.py:78
  120.0 0.0 reduce-scatter.7.cloned.1.call-update
  120.1 0.3 reduce-scatter.9.cloned.1.call-start
  120.3 37.9 %all-gather.7.cloned.1.call-done = bf16[512,1,1536]{2,0,1:T(8,128)(2,1)} async-done(((bf16[32,1,1536]{2,0,1:T(8,128)(2,1)}), bf16[512,1,1536]{2,0,1:T(8,128)(2,1)}) %all-gather.7.cloned.1.call-update) | async-done | bytes 1572880 | tf_op jit(solution)/shard_map/all_gather | solution.py:47
  158.2 6.8 %reshape.96 = bf16[16,32,4,8,48]{4,3,2,1,0:T(8,128)(2,1)} reshape(bf16[512,1,1536]{2,0,1:T(8,128)(2,1)} %all-gather.7.cloned.1.call-done) | data formatting | bytes 3145728 | tf_op jit(solution)/shard_map/reshape | solution.py:39
  165.0 3.5 fusion.8
  168.6 0.8 fusion.38
  169.3 1.3 convert_bitcast_fusion
  170.6 3.1 copy.82
  173.7 8.7 %convert_element_type.87 = bf16[16,32,1536]{2,1,0:T(8,128)(2,1)} reshape(bf16[16,32,4,8,48]{4,3,2,1,0:T(8,128)(2,1)} %copy.82) | data formatting | bytes 3145728 | tf_op jit(solution)/shard_map/convert_element_type | solution.py:81
  182.4 67.8 %reduce-scatter.7.cloned.1.call-done = bf16[1,32,1536]{2,1,0:T(8,128)(2,1)} async-done(((bf16[16,32,1536]{2,1,0:T(8,128)(2,1)}), bf16[1,32,1536]{2,1,0:T(8,128)(2,1)}) %reduce-scatter.7.cloned.1.call-update) | async-done | bytes 98320
  250.2 1.6 reduce.3
  251.7 0.7 reshape.158
  252.4 14.6 %all-to-all-start.1 = ((bf16[32,2,768]{2,1,0:T(2,128)(2,1)}), bf16[32,2,768]{2,1,0:T(2,128)(2,1)S(1)}, u32[]{:S(2)}, u32[]{:S(2)}) async-start(bf16[32,2,768]{2,1,0:T(2,128)(2,1)} %reshape.158), calls=%async_computation.1 | async-start | bytes 196608 | tf_op jit(solution)/shard_map/all_to_all | solution.py:87
  267.0 4.0 %bitcast_convert_fusion = bf16[4,192,16,48]{1,3,2,0:T(8,128)(2,1)S(1)} fusion(bf16[16,32,4,8,48]{4,3,2,1,0:T(8,128)(2,1)} %reshape.96, bf16[32,4,8,192,1]{3,2,0,1,4:T(8,128)(2,1)S(1)} %get-tuple-element.20), kind=kOutput, calls=%fused_computation.10 | convolution fusion | flops 302579712 | bytes 3145728 | tf_op jit(solution)/shard_map/sech,nsecf->ehnf/dot_general | solution.py:70
  271.1 71.5 %reduce-scatter.9.cloned.1.call-done = bf16[1,32,1536]{2,1,0:T(8,128)(2,1)} async-done(((bf16[16,32,1536]{2,1,0:T(8,128)(2,1)}), bf16[1,32,1536]{2,1,0:T(8,128)(2,1)}) %reduce-scatter.9.cloned.1.call-update) | async-done | bytes 98320
  342.6 1.6 reduce.5
  344.1 0.7 reshape.162
  344.8 14.6 %all-to-all-start.3 = ((bf16[32,2,768]{2,1,0:T(2,128)(2,1)}), bf16[32,2,768]{2,1,0:T(2,128)(2,1)S(1)}, u32[]{:S(2)}, u32[]{:S(2)}) async-start(bf16[32,2,768]{2,1,0:T(2,128)(2,1)} %reshape.162), calls=%async_computation.3 | async-start | bytes 196608 | tf_op jit(solution)/shard_map/all_to_all | solution.py:88
  359.4 4.2 %bitcast_convert_fusion.1 = bf16[4,16,48,192]{3,2,1,0:T(8,128)(2,1)S(1)} fusion(bf16[16,32,4,8,48]{4,3,2,1,0:T(8,128)(2,1)} %reshape.92, bf16[32,4,8,192,1]{3,2,0,1,4:T(8,128)(2,1)} %bitcast.113), kind=kOutput, calls=%fused_computation.11 | convolution fusion | flops 302579712 | bytes 3145728 | tf_op jit(solution)/shard_map/nsecf,sech->enfh/dot_general | solution.py:65
  363.6 1.5 copy.91
  365.1 1.5 copy.90
  366.5 0.1 reshape.159
  366.6 0.6 reduce
  367.2 0.2 reshape.95
  367.4 1.3 gather_fusion
  368.8 0.1 multiply_convert_fusion.1
  368.9 0.7 copy.88
  369.6 4.3 %all-to-all-done.3 = bf16[32,2,768]{2,1,0:T(2,128)(2,1)S(1)} async-done(((bf16[32,2,768]{2,1,0:T(2,128)(2,1)}), bf16[32,2,768]{2,1,0:T(2,128)(2,1)S(1)}, u32[]{:S(2)}, u32[]{:S(2)}) %all-to-all-start.3) | async-done | bytes 98336 | tf_op jit(solution)/shard_map/all_to_all | solution.py:88
  373.9 0.1 reshape.163
  374.0 0.6 reduce.1
  374.5 0.2 reshape.97
  374.8 1.3 gather_fusion.1
  376.1 0.7 copy.89
  (26 shorter events, 0.2 us)
Async XLA Ops:
  7.2 2.1 copy-start.5
  7.2 88.7 %all-gather.5.cloned.1.call-start = ((), (), s32[]{:S(2)}) async-start(), calls=%async_computation.6 | async-start | bytes 1671168 | tf_op jit(solution)/shard_map/all_gather | solution.py:46
  9.2 36.3 %copy-start.4 = (bf16[512,48]{0,1:T(8,128)(2,1)S(1)}, bf16[512,48]{0,1:T(8,128)(2,1)}, u32[]{:S(2)}) copy-start(bf16[512,48]{0,1:T(8,128)(2,1)} %param.11) | copy-start | bytes 147460
  9.3 36.5 %copy-start.6 = (f32[512,1]{0,1:T(1,128)S(1)}, f32[512,1]{0,1:T(1,128)}, u32[]{:S(2)}) copy-start(f32[512,1]{0,1:T(1,128)} %param.8) | copy-start | bytes 6148
  44.8 23.6 %copy-start.3 = (bf16[4,768,192]{1,2,0:T(8,128)(2,1)S(1)}, bf16[4,768,192]{1,2,0:T(8,128)(2,1)}, u32[]{:S(2)}) copy-start(bf16[4,768,192]{1,2,0:T(8,128)(2,1)} %param.9) | copy-start | bytes 3538948
  45.5 112.7 %all-gather.7.cloned.1.call-start = ((), (), s32[]{:S(2)}) async-start(), calls=%async_computation.7 | async-start | bytes 1671168 | tf_op jit(solution)/shard_map/all_gather | solution.py:47
  68.2 182.0 %reduce-scatter.7.cloned.1.call-start = ((), (), s32[]{:S(2)}) async-start(), calls=%async_computation.8 | async-start | bytes 1671168
  106.1 1.0 copy-start.1
  120.1 222.5 %reduce-scatter.9.cloned.1.call-start = ((), (), s32[]{:S(2)}) async-start(), calls=%async_computation.9 | async-start | bytes 1671168
  165.0 3.5 copy-start.2
  169.3 1.3 copy-start
  252.4 92.4 %all-to-all-start.1 = ((bf16[32,2,768]{2,1,0:T(2,128)(2,1)}), bf16[32,2,768]{2,1,0:T(2,128)(2,1)S(1)}, u32[]{:S(2)}, u32[]{:S(2)}) async-start(bf16[32,2,768]{2,1,0:T(2,128)(2,1)} %reshape.158), calls=%async_computation.1 | async-start | bytes 196608 | tf_op jit(solution)/shard_map/all_to_all | solution.py:87
  344.8 29.1 %all-to-all-start.3 = ((bf16[32,2,768]{2,1,0:T(2,128)(2,1)}), bf16[32,2,768]{2,1,0:T(2,128)(2,1)S(1)}, u32[]{:S(2)}, u32[]{:S(2)}) async-start(bf16[32,2,768]{2,1,0:T(2,128)(2,1)} %reshape.162), calls=%async_computation.3 | async-start | bytes 196608 | tf_op jit(solution)/shard_map/all_to_all | solution.py:88
Sparse Core Ops, SparseCore 0:
  45.7 50.1 all-gather.4
  99.5 58.7 all-gather.6
  162.3 87.7 reduce-scatter.6
  254.1 88.4 reduce-scatter.8
where the time goes:
time: 384 us; the launch traced here: 383 us
  waiting for transfers between devices  207 us (54%)
  local copies, waits for them, and re-layouts  55.7 us (15%)
  blocking collectives  49.5 us (13%)
  starting transfers between devices  29.8 us (8%)
  matrix products  17.7 us (5%)
  between operations  14.1 us (4%)
  other arithmetic  9.97 us (3%)
    unnamed x6, waiting for transfers between devices  139 us
    all_gather x1, waiting for transfers between devices, local(): lax.all_gather(arrived[1][None], 'hidden', axis=0, tiled=True)  37.9 us
    all_to_all x1, blocking collectives, local(): lax.all_to_all(to_slots(tokens), 'expert', split_axis=0, concat_axis=0, t...  31.3 us
    all_gather x1, waiting for transfers between devices, local(): lax.all_gather(arrived[0][None], 'hidden', axis=0, tiled=True)  25.1 us
    all_to_all x1, blocking collectives, local(): lax.all_to_all(to_slots(scaled), 'expert', split_axis=0, concat_axis=0, t...  18.2 us
    all_to_all x1, starting transfers between devices, local(): lax.all_to_all(grad_rows, 'expert', split_axis=0, concat_axis=0, tiled=True)  14.6 us
    all_to_all x1, starting transfers between devices, local(): lax.all_to_all(out_rows, 'expert', split_axis=0, concat_axis=0, tiled=True)  14.6 us
    reshape x2, local copies, waits for them, and re-layouts, by_expert(): return gathered.reshape(blocks, owners, exp_dev, capacity, features)  13.6 us
  transfers between devices with their start and end apart: 6, of which 5 were waited for; matrix products, arithmetic and copies ran while one was open for 19% of the time, Pallas kernels for 0%

commit v1 on v0

v1 whole, which is shorter than its diff:
```python
import functools

import jax
import jax.numpy as jnp
from jax import lax
from jax.experimental import pallas as pl
from jax.experimental.pallas import tpu as pltpu
from jax.sharding import PartitionSpec as P

MESH = pl.DeviceIdType.MESH
RING = 4
CORES = 2
CAP = 8
PAIR = 2
CHUNKS = 2
LANES = 128
F32 = jnp.float32
BF16 = jnp.bfloat16
NN = (((1,), (0,)), ((), ()))
NT = (((1,), (1,)), ((), ()))

PLACES = (0, -1, 1, 2)
ARRIVALS = [(-1, 0, None), (1, 0, None), (2, 0, 0), (2, 0, 1)]
for _i in PLACES:
    ARRIVALS += [(_i, -1, None), (_i, 1, None), (_i, 2, 0), (_i, 2, 1)]
ARRIVAL = {name: number for number, name in enumerate(ARRIVALS)}
ITEM = {2: 0, 1: 1, -1: 2, 0: 3}


def near(place):
    return (place + 1) % RING - 1


def dot(a, b, dims=NN):
    return lax.dot_general(a, b, dims, preferred_element_type=F32)


def gelu_and_slope(v):
    c = 0.7978845608028654
    square = v * v
    t = jnp.tanh(c * (v + 0.044715 * v * square))
    half = 0.5 * (1.0 + t)
    slope = half + 0.5 * v * (1.0 - t * t) * (c + c * 3.0 * 0.044715 * square)
    return v * half, slope


def kernel(
    tokens_ref, routes_ref, gate_ref, wint_ref, wout_ref, cot_ref,
    layer_ref, gtok_ref, gwint_ref, gwout_ref,
    chosen_v, send_v, recv_v, bsend_v, back_v, xg_v, part_v, via_v, frm_v,
    wint_v, wout_v, win_v, woutt_v, hid_v, gp_v, gwint_v, gwout_v,
    w_sem, gw_sem, a2a_send, a2a_recv, back_send, back_recv,
    ag_send, ag_recv, rs_send, via_recv, frm_recv,
):
    owners = lax.axis_size("expert")
    feat, tok = tokens_ref.shape
    exp_dev, units, width = wint_ref.shape
    rows = PAIR * CAP
    length = owners * rows
    half = length // 2
    chips = owners // CORES
    me = lax.axis_index("expert")
    here = lax.axis_index("hidden")
    x, y = here // RING, lax.rem(here, RING)

    def hidden_at(dx, dy):
        return lax.rem(x + dx + RING, RING) * RING + lax.rem(y + dy + RING, RING)

    def place(part, i, j):
        return hidden_at(i, j) if part == 0 else hidden_at(j, i)

    def neighbour(part, axis, step):
        return (me, place(part, step, 0) if axis == 0 else place(part, 0, step))

    wint_copy = pltpu.make_async_copy(wint_ref, wint_v, w_sem.at[0])
    wout_copy = pltpu.make_async_copy(wout_ref, wout_v, w_sem.at[1])
    wint_copy.start()
    wout_copy.start()
    barrier = pltpu.get_barrier_semaphore()

    def greet(i, carry):
        pl.semaphore_signal(barrier, inc=1, device_id=(lax.rem(me + i, owners), here), device_id_type=MESH)
        return carry

    lax.fori_loop(1, owners, greet, 0)
    for step in (1, -1):
        for axis in (0, 1):
            pl.semaphore_signal(barrier, inc=1, device_id=neighbour(0, axis, step), device_id_type=MESH)

    routes = routes_ref[...]
    experts = owners * exp_dev
    matches = jnp.where(routes == lax.broadcasted_iota(jnp.int32, (experts, tok), 0), 1.0, 0.0)
    earlier = jnp.where(
        lax.broadcasted_iota(jnp.int32, (tok, tok), 0) < lax.broadcasted_iota(jnp.int32, (tok, tok), 1), 1.0, 0.0
    ).astype(BF16)
    before = dot(matches.astype(BF16), earlier)
    slot = jnp.sum(before * matches, axis=0, keepdims=True).astype(jnp.int32)
    within = routes & (exp_dev - 1)
    pos = (within // PAIR) * length + (routes // exp_dev) * rows + (within & (PAIR - 1)) * CAP + slot
    scaled = gate_ref[...] * cot_ref[...].astype(F32)
    empty = jnp.zeros((LANES - 2 * feat, tok), BF16)
    both = jnp.concatenate([tokens_ref[...], scaled.astype(BF16), empty], axis=0)
    for p in range(CHUNKS):
        chosen_v[p] = jnp.where(
            lax.broadcasted_iota(jnp.int32, (length, tok), 0) + p * length == pos, 1.0, 0.0
        ).astype(BF16)
        send_v[p] = dot(chosen_v[p], both, NT).astype(BF16)

    pl.semaphore_wait(barrier, owners - 1 + 4)

    def exchange(src, dst, send_sem, recv_sem):
        def one(to):
            pltpu.make_async_remote_copy(
                src_ref=src.at[pl.ds(pl.multiple_of(to * rows, rows), rows)],
                dst_ref=dst.at[pl.ds(pl.multiple_of(me * rows, rows), rows)],
                send_sem=send_sem, recv_sem=recv_sem, device_id=(to, here), device_id_type=MESH,
            ).start()

        def chip(i, carry):
            distance = chips // 2 - (i + 1) // 2
            step = jnp.where(lax.rem(i, 2) == 1, distance, chips - distance)
            for other in range(CORES):
                one(lax.rem((me // CORES + step) * CORES + lax.rem(me + other, CORES), owners))
            return carry

        lax.fori_loop(0, chips - 1, chip, 0)
        one((me // CORES) * CORES + 1 - lax.rem(me, CORES))
        mine = pl.ds(pl.multiple_of(me * rows, rows), rows)
        dst[mine, :] = src[mine, :]

    def exchange_wait(ref, sem):
        view = ref.at[pl.ds(0, length - rows)]
        pltpu.make_async_copy(view, view, sem).wait()

    for p in range(CHUNKS):
        exchange(send_v.at[p], recv_v.at[p], a2a_send.at[p], a2a_recv.at[p])

    wint_copy.wait()
    wout_copy.wait()
    for e in range(exp_dev):
        win_v[e] = jnp.transpose(wint_v[e])
        woutt_v[e] = jnp.transpose(wout_v[e])

    def lanes_of(ref, which):
        return ref if which is None else ref.at[:, pl.ds(which * half, half)]

    def ag_copy(part, p, i, j, which, axis, step):
        ref = lanes_of(xg_v.at[part, p, place(part, i, j)], which)
        there = (near(i - step), j, which) if axis == 0 else (i, near(j - step), which)
        return pltpu.make_async_remote_copy(
            src_ref=ref, dst_ref=ref, send_sem=ag_send.at[part, p],
            recv_sem=ag_recv.at[part, p, ARRIVAL[there]],
            device_id=neighbour(part, axis, step), device_id_type=MESH,
        )

    def ag_send_to(part, p, i, j, which, axis, step):
        ag_copy(part, p, i, j, which, axis, step).start()

    def ag_wait(part, p, i, j, which=None):
        ref = lanes_of(xg_v.at[part, p, place(part, i, j)], which)
        pltpu.make_async_copy(ref, ref, ag_recv.at[part, p, ARRIVAL[(i, j, which)]]).wait()

    def ag_start(p):
        exchange_wait(recv_v.at[p], a2a_recv.at[p])
        arrived = recv_v[p].astype(F32).reshape(owners, PAIR, CAP, LANES)
        for e in range(PAIR):
            turned = jnp.transpose(arrived[:, e].reshape(half, LANES))
            for part in range(2):
                xg_v[part, p, here, :, e * half:(e + 1) * half] = turned[part * feat:(part + 1) * feat].astype(BF16)
        for axis in (0, 1):
            for step in (1, -1):
                for part in range(2):
                    ag_send_to(part, p, 0, 0, None, axis, step)

    def ag_first(p):
        for which, step in ((0, 1), (1, -1)):
            for part in range(2):
                ag_wait(part, p, -step, 0)
                ag_send_to(part, p, -step, 0, which, 0, step)
                for up in (1, -1):
                    ag_send_to(part, p, -step, 0, None, 1, up)

    def ag_row(p, i):
        for which, step in ((0, 1), (1, -1)):
            for part in range(2):
                ag_wait(part, p, i, -step)
                ag_send_to(part, p, i, -step, which, 1, step)

    def ag_second(p):
        for part in range(2):
            for which in range(2):
                ag_wait(part, p, 2, 0, which)
            for up in (1, -1):
                ag_send_to(part, p, 2, 0, None, 1, up)

    def ag_end(p):
        for i in PLACES:
            for part in range(2):
                for which in range(2):
                    ag_wait(part, p, i, 2, which)

    def forward_backward(p, e):
        expert = p * PAIR + e
        span = slice(e * half, (e + 1) * half)
        rows_x = xg_v[0, p, :, :, span].reshape(width, half)
        rows_g = xg_v[1, p, :, :, span].reshape(width, half)
        act, slope = gelu_and_slope(dot(wint_v[expert], rows_x))
        act = act.astype(BF16)
        hid_v[expert] = act
        part_v[0, p, :, :, span] = dot(woutt_v[expert], act).astype(BF16).reshape(width // feat, feat, half)
        grad = (dot(wout_v[expert], rows_g) * slope).astype(BF16)
        gp_v[expert] = grad
        part_v[1, p, :, :, span] = dot(win_v[expert], grad).astype(BF16).reshape(width // feat, feat, half)

    def weight_grads(p, e):
        expert = p * PAIR + e
        span = slice(e * half, (e + 1) * half)
        rows_x = xg_v[0, p, :, :, span].reshape(width, half)
        rows_g = xg_v[1, p, :, :, span].reshape(width, half)
        gwint_v[expert] = dot(gp_v[expert], rows_x, NT).astype(BF16)
        pltpu.make_async_copy(gwint_v.at[expert], gwint_ref.at[expert], gw_sem.at[0, expert]).start()
        gwout_v[expert] = dot(hid_v[expert], rows_g, NT).astype(BF16)
        pltpu.make_async_copy(gwout_v.at[expert], gwout_ref.at[expert], gw_sem.at[1, expert]).start()

    def rs_copy(part, p, i, j, which, axis, step, item, through):
        ref = lanes_of(part_v.at[part, p, place(part, i, j)], which)
        number = 0 if step == 1 else 1
        if through:
            dst, sem = via_v.at[part, p, item, number], via_recv.at[part, p, item, number]
        else:
            dst, sem = lanes_of(frm_v.at[part, p, item, number], which), frm_recv.at[part, p, item, number]
        pltpu.make_async_remote_copy(
            src_ref=ref, dst_ref=dst, send_sem=rs_send.at[part, p], recv_sem=sem,
            device_id=neighbour(part, axis, step), device_id_type=MESH,
        ).start()

    def rs_start(p, which):
        step = 1 if which == 0 else -1
        for i, item in ITEM.items():
            for part in range(2):
                rs_copy(part, p, i, 2, which, 1, step, item, True)
            for part in range(2):
                rs_copy(part, p, i, -step, which, 1, -step, item, False)

    def add_via(part, p, i, j, which, item):
        number = which
        buf = via_v.at[part, p, item, number]
        pltpu.make_async_copy(buf, buf, via_recv.at[part, p, item, number]).wait()
        ref = lanes_of(part_v.at[part, p, place(part, i, j)], which)
        ref[...] = (ref[...].astype(F32) + buf[...].astype(F32)).astype(BF16)

    def rs_middle(p, i):
        item = ITEM[i]
        for which, step in ((0, 1), (1, -1)):
            for part in range(2):
                add_via(part, p, i, step, which, item)
                rs_copy(part, p, i, step, which, 1, step, item, False)

    def total_of(part, p, i, item):
        total = part_v[part, p, place(part, i, 0)].astype(F32)
        for number in range(2):
            buf = frm_v.at[part, p, item, number]
            pltpu.make_async_copy(buf, buf, frm_recv.at[part, p, item, number]).wait()
            total = total + buf[...].astype(F32)
        return total.astype(BF16)

    def rs_sum(p, i):
        for part in range(2):
            part_v[part, p, place(part, i, 0)] = total_of(part, p, i, ITEM[i])
            if i == 2:
                rs_copy(part, p, i, 0, 0, 0, 1, 4, True)
                rs_copy(part, p, i, 0, 1, 0, -1, 4, True)
            elif i == 1:
                rs_copy(part, p, i, 0, 1, 0, 1, 4, False)
            elif i == -1:
                rs_copy(part, p, i, 0, 0, 0, -1, 4, False)

    def rs_last(p):
        for which, step in ((0, 1), (1, -1)):
            for part in range(2):
                add_via(part, p, step, 0, which, 4)
                rs_copy(part, p, step, 0, which, 0, step, 4, False)

    def rs_end(p):
        totals = [total_of(part, p, 0, 4).astype(F32) for part in range(2)]
        totals.append(jnp.zeros((LANES - 2 * feat, length), F32))
        turned = jnp.transpose(jnp.concatenate(totals, axis=0)).reshape(PAIR, owners, CAP, LANES)
        turned = jnp.concatenate([turned[e][:, None] for e in range(PAIR)], axis=1)
        bsend_v[p] = turned.reshape(length, LANES).astype(BF16)
        exchange(bsend_v.at[p], back_v.at[p], back_send.at[p], back_recv.at[p])

    ag_start(0)
    ag_first(0)
    ag_row(0, 0)
    ag_second(0)
    ag_row(0, -1)
    ag_start(1)
    ag_row(0, 1)
    ag_row(0, 2)
    ag_first(1)
    ag_row(1, 0)
    ag_second(1)
    ag_end(0)
    forward_backward(0, 0)
    rs_start(0, 0)
    ag_row(1, -1)
    ag_row(1, 1)
    ag_row(1, 2)
    forward_backward(0, 1)
    rs_start(0, 1)
    weight_grads(0, 0)
    weight_grads(0, 1)
    ag_end(1)
    forward_backward(1, 0)
    rs_start(1, 0)
    forward_backward(1, 1)
    rs_start(1, 1)
    for i in ITEM:
        rs_middle(0, i)
    for i in ITEM:
        rs_sum(0, i)
    weight_grads(1, 0)
    weight_grads(1, 1)
    rs_last(0)
    for i in ITEM:
        rs_middle(1, i)
    rs_end(0)
    for i in ITEM:
        rs_sum(1, i)
    rs_last(1)
    rs_end(1)

    taken = jnp.zeros((LANES, tok), F32)
    for p in range(CHUNKS):
        exchange_wait(back_v.at[p], back_recv.at[p])
        turned = jnp.transpose(back_v[p].astype(F32)).astype(BF16)
        taken = taken + dot(turned, chosen_v[p])
    layer_ref[...] = (gate_ref[...] * taken[0:feat]).astype(BF16)
    gtok_ref[...] = taken[feat:2 * feat].astype(BF16)

    for expert in range(exp_dev):
        pltpu.make_async_copy(gwint_v.at[expert], gwint_ref.at[expert], gw_sem.at[0, expert]).wait()
        pltpu.make_async_copy(gwout_v.at[expert], gwout_ref.at[expert], gw_sem.at[1, expert]).wait()
    for p in range(CHUNKS):
        exchange_wait(send_v.at[p], a2a_send.at[p])
        exchange_wait(bsend_v.at[p], back_send.at[p])
        for part in range(2):
            for buf, sem in ((xg_v, ag_send), (part_v, rs_send)):
                view = buf.at[part, p, pl.ds(0, RING * RING - 1)]
                pltpu.make_async_copy(view, view, sem.at[part, p]).wait()


def local(tokens, routes, gate_value, weight_in, weight_out, cotangent):
    owners = lax.axis_size("expert")
    blocks = lax.axis_size("hidden")
    tok, feat = tokens.shape
    exp_dev, width, units = weight_in.shape
    length = owners * PAIR * CAP
    half = length // 2
    vmem = pl.BlockSpec(memory_space=pltpu.VMEM)
    hbm = pl.BlockSpec(memory_space=pl.ANY)
    dma = pltpu.SemaphoreType.DMA
    weights = pltpu.VMEM((exp_dev, units, width), BF16)
    turned_weights = pltpu.VMEM((exp_dev, width, units), BF16)
    rows = pltpu.VMEM((CHUNKS, length, LANES), BF16)
    layer_out, grad_tokens, grad_in, grad_out = pl.pallas_call(
        kernel,
        out_shape=(
            jax.ShapeDtypeStruct((feat, tok), BF16),
            jax.ShapeDtypeStruct((feat, tok), BF16),
            jax.ShapeDtypeStruct((exp_dev, units, width), BF16),
            jax.ShapeDtypeStruct((exp_dev, units, width), BF16),
        ),
        in_specs=[vmem, vmem, vmem, hbm, hbm, vmem],
        out_specs=(vmem, vmem, hbm, hbm),
        scratch_shapes=[
            pltpu.VMEM((CHUNKS, length, tok), BF16),
            rows, rows, rows, rows,
            pltpu.VMEM((2, CHUNKS, blocks, feat, length), BF16),
            pltpu.VMEM((2, CHUNKS, blocks, feat, length), BF16),
            pltpu.VMEM((2, CHUNKS, 5, 2, feat, half), BF16),
            pltpu.VMEM((2, CHUNKS, 5, 2, feat, length), BF16),
            weights, weights, turned_weights, turned_weights,
            pltpu.VMEM((exp_dev, units, half), BF16),
            pltpu.VMEM((exp_dev, units, half), BF16),
            weights, weights,
            dma((2,)),
            dma((2, exp_dev)),
            dma((CHUNKS,)),
            dma((CHUNKS,)),
            dma((CHUNKS,)),
            dma((CHUNKS,)),
            dma((2, CHUNKS)),
            dma((2, CHUNKS, len(ARRIVALS))),
            dma((2, CHUNKS)),
            dma((2, CHUNKS, 5, 2)),
            dma((2, CHUNKS, 5, 2)),
        ],
        compiler_params=pltpu.CompilerParams(
            collective_id=0, has_side_effects=True, vmem_limit_bytes=60 * 1024 * 1024
        ),
        name="expert_layer",
    )(tokens.T, routes.T, gate_value.T, weight_in.transpose(0, 2, 1), weight_out, cotangent.T)
    return layer_out.T, grad_tokens.T, grad_in.transpose(0, 2, 1), grad_out


def solution(mesh):
    in_specs = (
        P("expert", "hidden"),
        P("expert", None),
        P("expert", None),
        P("expert", None, "hidden"),
        P("expert", "hidden", None),
        P("expert", "hidden"),
    )
    out_specs = (
        P("expert", "hidden"),
        P("expert", "hidden"),
        P("expert", None, "hidden"),
        P("expert", "hidden", None),
    )
    return jax.shard_map(local, mesh=mesh, in_specs=in_specs, out_specs=out_specs, check_vma=False)
```

time: 384 us -> 93.3 us (0.24)
  waiting for transfers between devices: 207 us -> 0 us
  Pallas kernels: 0 us -> 86 us
  blocking collectives: 49.5 us -> 0 us
  local copies, waits for them, and re-layouts: 55.7 us -> 6.31 us
  starting transfers between devices: 29.8 us -> 0 us
  matrix products: 17.7 us -> 0 us
  between operations: 14.1 us -> 0.64 us
  other arithmetic: 9.97 us -> 0 us
    unnamed x6 -> x0, waiting for transfers between devices: 139 us -> none
    pallas_call x0 -> x1, Pallas kernels: none -> 86 us  [local(): pl.pallas_call(kernel, out_shape=(jax.ShapeDtypeStruct((feat, tok), BF16)...]
    all_gather x2 -> x0, waiting for transfers between devices: 63 us -> none  [the longest x1 37.9 us: local(): lax.all_gather(arrived[1][None], 'hidden', axis=0, tiled=True)]
    all_to_all x2 -> x0, blocking collectives: 49.5 us -> none  [the longest x1 31.3 us: local(): lax.all_to_all(to_slots(tokens), 'expert', split_axis=0, concat_axis=0, t...]
    all_to_all x2 -> x0, starting transfers between devices: 29.2 us -> none  [the longest x1 14.6 us: local(): lax.all_to_all(grad_rows, 'expert', split_axis=0, concat_axis=0, tiled=True)]
    convert_element_type x4 -> x0, local copies, waits for them, and re-layouts: 23.4 us -> none  [the longest x2 11.7 us: local(): flat_grad.astype(jnp.bfloat16)]
    dot_general x6 -> x0, matrix products: 17.7 us -> none  [the longest x1 4.16 us: local(): jnp.einsum('nsecf,sech->enfh', rows_x, grad_pre, preferred_element_type=j...]
    reshape x4 -> x0, local copies, waits for them, and re-layouts: 14.1 us -> none  [the longest x2 13.6 us: by_expert(): return gathered.reshape(blocks, owners, exp_dev, capacity, features)]
  transfers between devices with their start and end apart: 6 -> 0, of which waited for: 5 -> 0; matrix products, arithmetic and copies ran while one was open for 19% -> 0% of each run, Pallas kernels for 0% -> 0%
where the time goes in v1:
time: 93.3 us; the launch traced here: 93 us
  Pallas kernels  86 us (92%)
  local copies, waits for them, and re-layouts  6.31 us (7%)
    pallas_call x1, Pallas kernels, local(): pl.pallas_call(kernel, out_shape=(jax.ShapeDtypeStruct((feat, tok), BF16)...  86 us
    unnamed x6, local copies, waits for them, and re-layouts  6.31 us

profile of v1, /device:TPU:1, one launch (start us, length us, event | category | flops | bytes accessed | tf_op | source)
XLA Modules:
  0.0 93.0 jit_solution(8234658673967222749)
XLA Ops:
  0.6 86.0 %expert_layer.1 = (bf16[48,512]{1,0:T(8,128)(2,1)}, bf16[48,512]{1,0:T(8,128)(2,1)}, bf16[4,192,768]{2,1,0:T(8,128)(2,1)}, bf16[4,192,768]{2,1,0:T(8,128)(2,1)}) custom-call(bf16[48,512]{1,0:T(8,128)(2,1)} %bitcast.12, s32[1,512]{1,0:T(1,128)} %bitcast.14, f32[1,512]{1,0:T(1,128)} %bitcast.15, bf16[4,192,768]{2,1,0:T(8,128)(2,1)} %bitcast.8, ...), custom_call_target="tpu_custom_call" | custom-call | tf_op jit(solution)/shard_map/expert_layer/pallas_call | solution.py:366
  86.6 1.4 %copy.14 = bf16[512,48]{0,1:T(8,128)(2,1)} copy(bf16[512,48]{0,1:T(8,128)(2,1)} %bitcast.11) | data formatting | bytes 98304
  88.1 1.4 %copy.15 = bf16[512,48]{0,1:T(8,128)(2,1)} copy(bf16[512,48]{0,1:T(8,128)(2,1)} %bitcast.10) | data formatting | bytes 98304
  89.5 0.0 copy-start
  89.5 2.5 %copy.16 = bf16[4,768,192]{1,2,0:T(8,128)(2,1)} copy(bf16[4,768,192]{1,2,0:T(8,128)(2,1)} %bitcast.9) | data formatting | bytes 2359296
  91.9 0.0 copy-done
  91.9 1.0 %copy.17 = bf16[4,192,768]{2,1,0:T(8,128)(2,1)} copy(bf16[4,192,768]{2,1,0:T(8,128)(2,1)S(1)} %copy-done) | data formatting | bytes 2359296
Async XLA Ops:
  89.5 2.5 %copy-start = (bf16[4,192,768]{2,1,0:T(8,128)(2,1)S(1)}, bf16[4,192,768]{2,1,0:T(8,128)(2,1)}, u32[]{:S(2)}) copy-start(bf16[4,192,768]{2,1,0:T(8,128)(2,1)} %get-tuple-element.19) | copy-start | bytes 3538948

commit v2 on v1

v2 whole, which is shorter than its diff:
```python
import functools

import jax
import jax.numpy as jnp
from jax import lax
from jax.experimental import pallas as pl
from jax.experimental.pallas import tpu as pltpu
from jax.sharding import PartitionSpec as P

MESH = pl.DeviceIdType.MESH
RING = 4
CORES = 2
CAP = 8
PAIR = 2
SIDES = 2
CHUNKS = 4
LANES = 128
F32 = jnp.float32
BF16 = jnp.bfloat16
NN = (((1,), (0,)), ((), ()))
NT = (((1,), (1,)), ((), ()))

PLACES = (0, -1, 1, 2)
ARRIVALS = [(-1, 0, None), (1, 0, None), (2, 0, None)]
for _i in PLACES:
    ARRIVALS += [(_i, -1, None), (_i, 1, None), (_i, 2, 0), (_i, 2, 1)]
ARRIVAL = {name: number for number, name in enumerate(ARRIVALS)}
ITEM = {2: 0, 1: 1, -1: 2, 0: 3}

ORDER = (
    ("S", 0), ("S", 1), ("F", 0, -1), ("F", 0, 1), ("R", 0, 0), ("F", 0, 2), ("F", 1, -1), ("F", 1, 1),
    ("S", 2), ("R", 1, 0), ("F", 1, 2), ("R", 0, -1), ("R", 0, 1), ("R", 0, 2), ("R", 1, -1), ("R", 1, 1),
    ("F", 2, -1), ("S", 3), ("F", 2, 1), ("R", 2, 0), ("F", 2, 2), ("R", 1, 2), ("R", 2, -1), ("F", 3, -1),
    ("F", 3, 1), ("R", 3, 0), ("F", 3, 2), ("R", 2, 1), ("R", 2, 2), ("C", 1, 0), ("C", 1, 1), ("R", 3, -1),
    ("R", 3, 1), ("R", 3, 2), ("C", 2, 0), ("C", 2, 1), ("M", 1, 2), ("M", 1, 1), ("M", 1, -1), ("M", 1, 0),
    ("C", 3, 0), ("C", 3, 1), ("M", 2, 2), ("M", 2, 1), ("M", 2, -1), ("M", 2, 0), ("U", 1, 2), ("U", 1, 1),
    ("U", 1, -1), ("C", 0, 0), ("C", 0, 1), ("M", 3, 1), ("M", 3, -1), ("M", 3, 2), ("M", 3, 0), ("U", 2, 2),
    ("U", 2, 1), ("U", 2, -1), ("Z", 1), ("M", 0, 2), ("M", 0, 1), ("M", 0, -1), ("M", 0, 0), ("U", 3, 1),
    ("U", 3, -1), ("U", 3, 2), ("Z", 2), ("U", 0, 2), ("U", 0, 1), ("U", 0, -1), ("Z", 3), ("Z", 0),
)


def near(place):
    return (place + 1) % RING - 1


def dot(a, b, dims=NN):
    return lax.dot_general(a, b, dims, preferred_element_type=F32)


def gelu_and_slope(v):
    c = 0.7978845608028654
    square = v * v
    t = jnp.tanh(c * (v + 0.044715 * v * square))
    half = 0.5 * (1.0 + t)
    slope = half + 0.5 * v * (1.0 - t * t) * (c + c * 3.0 * 0.044715 * square)
    return v * half, slope


def kernel(
    tokens_ref, routes_ref, gate_ref, wint_ref, wout_ref, cot_ref,
    layer_ref, gtok_ref, gwint_ref, gwout_ref,
    chosen_v, send_v, recv_v, bsend_v, back_v, xg_v, part_v, via_v, frm_v, last_v,
    wint_v, wout_v, win_v, woutt_v, hid_v, gp_v, gwint_v, gwout_v,
    w_sem, gw_sem, a2a_send, a2a_recv, back_send, back_recv,
    ag_send, ag_recv, rs_send, via_recv, frm_recv, last_recv,
):
    owners = lax.axis_size("expert")
    feat, tok = tokens_ref.shape
    exp_dev, units, width = wint_ref.shape
    rows = PAIR * CAP
    length = owners // SIDES * rows
    half = length // PAIR
    chips = owners // CORES
    behind = max(chips // 4 - 1, 0)
    me = lax.axis_index("expert")
    here = lax.axis_index("hidden")
    x, y = here // RING, lax.rem(here, RING)

    def hidden_at(dx, dy):
        return lax.rem(x + dx + RING, RING) * RING + lax.rem(y + dy + RING, RING)

    def place(part, i, j):
        return hidden_at(i, j) if part == 0 else hidden_at(j, i)

    def neighbour(part, axis, step):
        return (me, place(part, step, 0) if axis == 0 else place(part, 0, step))

    wint_copy = pltpu.make_async_copy(wint_ref, wint_v, w_sem.at[0])
    wout_copy = pltpu.make_async_copy(wout_ref, wout_v, w_sem.at[1])
    wint_copy.start()
    wout_copy.start()
    barrier = pltpu.get_barrier_semaphore()

    def greet(i, carry):
        pl.semaphore_signal(barrier, inc=1, device_id=(lax.rem(me + i, owners), here), device_id_type=MESH)
        return carry

    lax.fori_loop(1, owners, greet, 0)
    for step in (1, -1, 2):
        for axis in (0, 1):
            pl.semaphore_signal(barrier, inc=1, device_id=neighbour(0, axis, step), device_id_type=MESH)

    routes = routes_ref[...]
    experts = owners * exp_dev
    matches = jnp.where(routes == lax.broadcasted_iota(jnp.int32, (experts, tok), 0), 1.0, 0.0)
    earlier = jnp.where(
        lax.broadcasted_iota(jnp.int32, (tok, tok), 0) < lax.broadcasted_iota(jnp.int32, (tok, tok), 1), 1.0, 0.0
    ).astype(BF16)
    before = dot(matches.astype(BF16), earlier)
    slot = jnp.sum(before * matches, axis=0, keepdims=True).astype(jnp.int32)
    pos = routes * CAP + slot
    scaled = gate_ref[...] * cot_ref[...].astype(F32)
    empty = jnp.zeros((LANES - 2 * feat, tok), BF16)
    both = jnp.concatenate([tokens_ref[...], scaled.astype(BF16), empty], axis=0)
    chosen_v[...] = jnp.where(
        lax.broadcasted_iota(jnp.int32, chosen_v.shape, 0) == pos, 1.0, 0.0
    ).astype(BF16)
    send_v[...] = dot(chosen_v[...], both, NT).astype(BF16)

    pl.semaphore_wait(barrier, owners - 1 + 6)

    chip, core = me // CORES, lax.rem(me, CORES)
    side_chips = chips // SIDES
    pairs = exp_dev // PAIR

    def block(number):
        return pl.ds(pl.multiple_of(number * rows, rows), rows)

    def exchange(c, outward, src, dst, send_sem, recv_sem):
        side, pair = c // pairs, c % pairs
        for number in sorted(
            range(side_chips), key=lambda k: -min((side * side_chips + k - behind) % chips, (behind - side * side_chips - k) % chips)
        ):
            ahead = side * side_chips + number - behind
            way = -ahead if outward else ahead
            for other in range(CORES):
                to_core = lax.rem(core + other, CORES)
                to = lax.rem(chip + way + chips, chips) * CORES + to_core
                if outward:
                    take, put = to * pairs + pair, (c * side_chips + number) * CORES + core
                else:
                    take, put = (c * side_chips + number) * CORES + to_core, me * pairs + pair
                if ahead == 0 and other == 0:
                    dst[block(put), :] = src[block(take), :]
                else:
                    pltpu.make_async_remote_copy(
                        src_ref=src.at[block(take)], dst_ref=dst.at[block(put)],
                        send_sem=send_sem.at[c], recv_sem=recv_sem.at[c], device_id=(to, here), device_id_type=MESH,
                    ).start()

    def exchange_wait(c, ref, sem):
        view = ref.at[pl.ds(0, length - rows if c // pairs == 0 else length)]
        pltpu.make_async_copy(view, view, sem.at[c]).wait()

    for c in range(CHUNKS):
        exchange(c, True, send_v, recv_v, a2a_send, a2a_recv)

    wint_copy.wait()
    wout_copy.wait()
    for e in range(exp_dev):
        win_v[e] = jnp.transpose(wint_v[e])
        woutt_v[e] = jnp.transpose(wout_v[e])

    def lanes_of(ref, which):
        return ref if which is None else ref.at[:, pl.ds(which * half, half)]

    def ag_copy(part, p, i, j, which, axis, step):
        ref = lanes_of(xg_v.at[part, p, place(part, i, j)], which)
        there = (near(i - step), j, which) if axis == 0 else (i, near(j - step), which)
        return pltpu.make_async_remote_copy(
            src_ref=ref, dst_ref=ref, send_sem=ag_send.at[part, p],
            recv_sem=ag_recv.at[part, p, ARRIVAL[there]],
            device_id=neighbour(part, axis, step), device_id_type=MESH,
        )

    def ag_send_to(part, p, i, j, which, axis, step):
        ag_copy(part, p, i, j, which, axis, step).start()

    def ag_wait(part, p, i, j, which=None):
        ref = lanes_of(xg_v.at[part, p, place(part, i, j)], which)
        pltpu.make_async_copy(ref, ref, ag_recv.at[part, p, ARRIVAL[(i, j, which)]]).wait()

    def ag_start(p):
        exchange_wait(p, recv_v, a2a_recv)
        arrived = recv_v[p * length:(p + 1) * length].astype(F32).reshape(length // rows, PAIR, CAP, LANES)
        for e in range(PAIR):
            turned = jnp.transpose(arrived[:, e].reshape(half, LANES))
            for part in range(2):
                xg_v[part, p, here, :, e * half:(e + 1) * half] = turned[part * feat:(part + 1) * feat].astype(BF16)
        for axis, step in ((0, 1), (0, -1), (0, 2), (1, 1), (1, -1)):
            for part in range(2):
                ag_send_to(part, p, 0, 0, None, axis, step)

    def ag_column(p, i):
        for part in range(2):
            ag_wait(part, p, i, 0)
            for step in (1, -1):
                ag_send_to(part, p, i, 0, None, 1, step)

    def ag_row(p, i):
        for which, step in ((0, 1), (1, -1)):
            for part in range(2):
                ag_wait(part, p, i, -step)
                ag_send_to(part, p, i, -step, which, 1, step)

    def ag_end(p):
        for i in PLACES:
            for part in range(2):
                for which in range(2):
                    ag_wait(part, p, i, 2, which)

    def rows_of(part, p, which):
        return xg_v[part, p, :, :, which * half:(which + 1) * half].reshape(width, half)

    def forward_backward(p, which):
        side, e = p // pairs, p % pairs * PAIR + which
        at, own = slice(which * half, (which + 1) * half), slice(side * half, (side + 1) * half)
        act, slope = gelu_and_slope(dot(wint_v[e], rows_of(0, p, which)))
        act = act.astype(BF16)
        hid_v[e, :, own] = act
        part_v[0, p, :, :, at] = dot(woutt_v[e], act).astype(BF16).reshape(width // feat, feat, half)
        grad = (dot(wout_v[e], rows_of(1, p, which)) * slope).astype(BF16)
        gp_v[e, :, own] = grad
        part_v[1, p, :, :, at] = dot(win_v[e], grad).astype(BF16).reshape(width // feat, feat, half)

    def weight_grads(e):
        rows_x, rows_g = [
            jnp.concatenate([rows_of(part, side * pairs + e // PAIR, e % PAIR) for side in range(SIDES)], axis=1)
            for part in range(2)
        ]
        gwint_v[e] = dot(gp_v[e], rows_x, NT).astype(BF16)
        pltpu.make_async_copy(gwint_v.at[e], gwint_ref.at[e], gw_sem.at[0, e]).start()
        gwout_v[e] = dot(hid_v[e], rows_g, NT).astype(BF16)
        pltpu.make_async_copy(gwout_v.at[e], gwout_ref.at[e], gw_sem.at[1, e]).start()

    def rs_copy(part, p, i, j, which, axis, step, dst, sem):
        pltpu.make_async_remote_copy(
            src_ref=lanes_of(part_v.at[part, p, place(part, i, j)], which), dst_ref=dst,
            send_sem=rs_send.at[part, p], recv_sem=sem,
            device_id=neighbour(part, axis, step), device_id_type=MESH,
        ).start()

    def rs_through(part, p, i, which, step):
        rs_copy(part, p, i, 2, which, 1, step, via_v.at[part, p, ITEM[i], which], via_recv.at[part, p, ITEM[i], which])

    def rs_to(part, p, i, which, step):
        number = 0 if step == 1 else 1
        dst = lanes_of(frm_v.at[part, p, ITEM[i], number], which)
        rs_copy(part, p, i, step, which, 1, step, dst, frm_recv.at[part, p, ITEM[i], number])

    def rs_start(p, which):
        step = 1 if which == 0 else -1
        for i in ITEM:
            for part in range(2):
                rs_through(part, p, i, which, step)
        for i in ITEM:
            for part in range(2):
                rs_to(part, p, i, which, -step)

    def rs_middle(p, i):
        for which, step in ((0, 1), (1, -1)):
            for part in range(2):
                buf, sem = via_v.at[part, p, ITEM[i], which], via_recv.at[part, p, ITEM[i], which]
                pltpu.make_async_copy(buf, buf, sem).wait()
                ref = lanes_of(part_v.at[part, p, place(part, i, step)], which)
                ref[...] = (ref[...].astype(F32) + buf[...].astype(F32)).astype(BF16)
                rs_to(part, p, i, which, step)

    def rs_total(part, p, i):
        total = part_v[part, p, place(part, i, 0)].astype(F32)
        for number in range(2):
            buf = frm_v.at[part, p, ITEM[i], number]
            pltpu.make_async_copy(buf, buf, frm_recv.at[part, p, ITEM[i], number]).wait()
            total = total + buf[...].astype(F32)
        return total

    def rs_sum(p, i):
        for part in range(2):
            part_v[part, p, place(part, i, 0)] = rs_total(part, p, i).astype(BF16)
            rs_copy(part, p, i, 0, None, 0, i, last_v.at[part, p, ITEM[i]], last_recv.at[part, p, ITEM[i]])

    def rs_last(part, p):
        total = rs_total(part, p, 0)
        for i in (1, -1, 2):
            buf = last_v.at[part, p, ITEM[i]]
            pltpu.make_async_copy(buf, buf, last_recv.at[part, p, ITEM[i]]).wait()
            total = total + buf[...].astype(F32)
        return total.astype(BF16).astype(F32)

    def rs_end(p):
        totals = [rs_last(part, p) for part in range(2)]
        totals.append(jnp.zeros((LANES - 2 * feat, length), F32))
        turned = jnp.transpose(jnp.concatenate(totals, axis=0)).reshape(PAIR, length // rows, CAP, LANES)
        turned = jnp.concatenate([turned[e][:, None] for e in range(PAIR)], axis=1)
        bsend_v[p * length:(p + 1) * length] = turned.reshape(length, LANES).astype(BF16)
        exchange(p, False, bsend_v, back_v, back_send, back_recv)

    def compute(p, which):
        if which == 0:
            ag_end(p)
        forward_backward(p, which)
        rs_start(p, which)

    for step, *on in ORDER:
        {"S": ag_start, "F": ag_column, "R": ag_row, "C": compute, "M": rs_middle, "U": rs_sum, "Z": rs_end}[step](*on)
    for e in range(exp_dev):
        weight_grads(e)

    for p in range(CHUNKS):
        exchange_wait(p, back_v, back_recv)
    turned = jnp.transpose(back_v[...].astype(F32)).astype(BF16)
    taken = dot(turned, chosen_v[...])
    layer_ref[...] = (gate_ref[...] * taken[0:feat]).astype(BF16)
    gtok_ref[...] = taken[feat:2 * feat].astype(BF16)

    for expert in range(exp_dev):
        pltpu.make_async_copy(gwint_v.at[expert], gwint_ref.at[expert], gw_sem.at[0, expert]).wait()
        pltpu.make_async_copy(gwout_v.at[expert], gwout_ref.at[expert], gw_sem.at[1, expert]).wait()
    for p in range(CHUNKS):
        exchange_wait(p, send_v, a2a_send)
        exchange_wait(p, bsend_v, back_send)
        for part in range(2):
            for buf, sem in ((xg_v, ag_send), (part_v, rs_send)):
                view = buf.at[part, p, pl.ds(0, RING * RING - 1)]
                pltpu.make_async_copy(view, view, sem.at[part, p]).wait()


def hand_over(*refs):
    count = (len(refs) - 2) // 3
    given, outs, held = refs[:count], refs[count:2 * count], refs[2 * count:3 * count]
    in_sem, out_sem = refs[3 * count:]
    into = [pltpu.make_async_copy(given[i], held[i], in_sem.at[i]) for i in range(count)]
    out = [pltpu.make_async_copy(held[i], outs[i], out_sem.at[i]) for i in range(count)]
    for copy in into:
        copy.start()
    for i in range(count):
        into[i].wait()
        out[i].start()
    for copy in out:
        copy.wait()


def local(tokens, routes, gate_value, weight_in, weight_out, cotangent):
    owners = lax.axis_size("expert")
    blocks = lax.axis_size("hidden")
    tok, feat = tokens.shape
    exp_dev, width, units = weight_in.shape
    slots = owners * exp_dev * CAP
    length = owners // SIDES * PAIR * CAP
    half = length // PAIR
    vmem = pl.BlockSpec(memory_space=pltpu.VMEM)
    hbm = pl.BlockSpec(memory_space=pl.ANY)
    dma = pltpu.SemaphoreType.DMA
    weights = pltpu.VMEM((exp_dev, units, width), BF16)
    turned_weights = pltpu.VMEM((exp_dev, width, units), BF16)
    rows = pltpu.VMEM((slots, LANES), BF16)
    outs = pl.pallas_call(
        kernel,
        out_shape=(
            jax.ShapeDtypeStruct((feat, tok), BF16),
            jax.ShapeDtypeStruct((feat, tok), BF16),
            jax.ShapeDtypeStruct((exp_dev, units, width), BF16),
            jax.ShapeDtypeStruct((exp_dev, units, width), BF16),
        ),
        in_specs=[vmem, vmem, vmem, hbm, hbm, vmem],
        out_specs=(vmem, vmem, hbm, hbm),
        scratch_shapes=[
            pltpu.VMEM((slots, tok), BF16),
            rows, rows, rows, rows,
            pltpu.VMEM((2, CHUNKS, blocks, feat, length), BF16),
            pltpu.VMEM((2, CHUNKS, blocks, feat, length), BF16),
            pltpu.VMEM((2, CHUNKS, RING, 2, feat, half), BF16),
            pltpu.VMEM((2, CHUNKS, RING, 2, feat, length), BF16),
            pltpu.VMEM((2, CHUNKS, RING - 1, feat, length), BF16),
            weights, weights, turned_weights, turned_weights,
            pltpu.VMEM((exp_dev, units, slots // exp_dev), BF16),
            pltpu.VMEM((exp_dev, units, slots // exp_dev), BF16),
            weights, weights,
            dma((2,)),
            dma((2, exp_dev)),
            dma((CHUNKS,)),
            dma((CHUNKS,)),
            dma((CHUNKS,)),
            dma((CHUNKS,)),
            dma((2, CHUNKS)),
            dma((2, CHUNKS, len(ARRIVALS))),
            dma((2, CHUNKS)),
            dma((2, CHUNKS, RING, 2)),
            dma((2, CHUNKS, RING, 2)),
            dma((2, CHUNKS, RING - 1)),
        ],
        compiler_params=pltpu.CompilerParams(
            collective_id=0, has_side_effects=True, vmem_limit_bytes=60 * 1024 * 1024
        ),
        name="expert_layer",
    )(tokens.T, routes.T, gate_value.T, weight_in.transpose(0, 2, 1), weight_out, cotangent.T)
    layer_out, grad_tokens, grad_in, grad_out = pl.pallas_call(
        hand_over,
        out_shape=tuple(jax.ShapeDtypeStruct(out.shape, out.dtype) for out in outs),
        in_specs=[hbm] * len(outs),
        out_specs=(hbm,) * len(outs),
        scratch_shapes=[pltpu.VMEM(out.shape, out.dtype) for out in outs] + [dma((len(outs),)), dma((len(outs),))],
        compiler_params=pltpu.CompilerParams(vmem_limit_bytes=60 * 1024 * 1024),
        name="hand_over",
    )(*outs)
    return layer_out.T, grad_tokens.T, grad_in.transpose(0, 2, 1), grad_out


def solution(mesh):
    in_specs = (
        P("expert", "hidden"),
        P("expert", None),
        P("expert", None),
        P("expert", None, "hidden"),
        P("expert", "hidden", None),
        P("expert", "hidden"),
    )
    out_specs = (
        P("expert", "hidden"),
        P("expert", "hidden"),
        P("expert", None, "hidden"),
        P("expert", "hidden", None),
    )
    return jax.shard_map(local, mesh=mesh, in_specs=in_specs, out_specs=out_specs, check_vma=False)
```

time: 93.3 us -> 81.9 us (0.88)
  local copies, waits for them, and re-layouts: 6.31 us -> 0 us
  Pallas kernels: 86 us -> 81 us
    pallas_call x1, Pallas kernels: 86 us -> 78.2 us  [local(): pl.pallas_call(kernel, out_shape=(jax.ShapeDtypeStruct((feat, tok), BF16)...]
    unnamed x6 -> x0, local copies, waits for them, and re-layouts: 6.31 us -> none
    pallas_call x0 -> x1, Pallas kernels: none -> 2.8 us  [local(): pl.pallas_call(hand_over, out_shape=tuple((jax.ShapeDtypeStruct(out.shape...]
where the time goes in v2:
time: 81.9 us; the launch traced here: 81.7 us
  Pallas kernels  81 us (99%)
    pallas_call x1, Pallas kernels, local(): pl.pallas_call(kernel, out_shape=(jax.ShapeDtypeStruct((feat, tok), BF16)...  78.2 us
    pallas_call x1, Pallas kernels, local(): pl.pallas_call(hand_over, out_shape=tuple((jax.ShapeDtypeStruct(out.shape...  2.8 us

profile of v2, /device:TPU:1, one launch (start us, length us, event | category | flops | bytes accessed | tf_op | source)
XLA Modules:
  0.0 81.7 jit_solution(85251541647424510)
XLA Ops:
  0.6 78.2 %expert_layer.1 = (bf16[48,512]{1,0:T(8,128)(2,1)}, bf16[48,512]{1,0:T(8,128)(2,1)}, bf16[4,192,768]{2,1,0:T(8,128)(2,1)}, bf16[4,192,768]{2,1,0:T(8,128)(2,1)}) custom-call(bf16[48,512]{1,0:T(8,128)(2,1)} %bitcast.9, s32[1,512]{1,0:T(1,128)} %bitcast.11, f32[1,512]{1,0:T(1,128)} %bitcast.12, bf16[4,192,768]{2,1,0:T(8,128)(2,1)} %bitcast.8, ...), custom_call_target="tpu_custom_call" | custom-call | tf_op jit(solution)/shard_map/expert_layer/pallas_call | solution.py:358
  78.9 2.8 %hand_over.1 = (bf16[48,512]{1,0:T(8,128)(2,1)}, bf16[48,512]{1,0:T(8,128)(2,1)}, bf16[4,192,768]{2,1,0:T(8,128)(2,1)}, bf16[4,192,768]{2,1,0:T(8,128)(2,1)}) custom-call(bf16[48,512]{1,0:T(8,128)(2,1)} %get-tuple-element.12.refs_0_, bf16[48,512]{1,0:T(8,128)(2,1)} %get-tuple-element.13.refs_1_, bf16[4,192,768]{2,1,0:T(8,128)(2,1)} %get-tuple-element.14.refs_2_, ...), custom_call_target="tpu_custom_call" | custom-call | tf_op jit(solution)/shard_map/hand_over/pallas_call | solution.py:398

commit v3 on v2

--- a/solution.py
+++ b/solution.py
@@ -38,6 +38,7 @@
     ("U", 2, 1), ("U", 2, -1), ("Z", 1), ("M", 0, 2), ("M", 0, 1), ("M", 0, -1), ("M", 0, 0), ("U", 3, 1),
     ("U", 3, -1), ("U", 3, 2), ("Z", 2), ("U", 0, 2), ("U", 0, 1), ("U", 0, -1), ("Z", 3), ("Z", 0),
 )
+BACK = [_step[1] for _step in ORDER if _step[0] == "Z"]
 
 
 def near(place):
@@ -58,23 +59,26 @@
 
 
 def kernel(
-    tokens_ref, routes_ref, gate_ref, wint_ref, wout_ref, cot_ref,
+    tokens_hbm, routes_hbm, gate_hbm, wint_ref, wout_ref, cot_hbm,
     layer_ref, gtok_ref, gwint_ref, gwout_ref,
-    chosen_v, send_v, recv_v, bsend_v, back_v, xg_v, part_v, via_v, frm_v, last_v,
+    tokens_ref, routes_ref, gate_ref, cot_ref, chosen_v, send_v, recv_v, bsend_v, back_v, xg_v, part_v, via_v, frm_v, last_v,
     wint_v, wout_v, win_v, woutt_v, hid_v, gp_v, gwint_v, gwout_v,
-    w_sem, gw_sem, a2a_send, a2a_recv, back_send, back_recv,
+    in_sem, w_sem, gw_sem, a2a_send, a2a_recv, back_send, back_recv,
     ag_send, ag_recv, rs_send, via_recv, frm_recv, last_recv,
 ):
     owners = lax.axis_size("expert")
-    feat, tok = tokens_ref.shape
+    feat, tok = tokens_hbm.shape
     exp_dev, units, width = wint_ref.shape
     rows = PAIR * CAP
     length = owners // SIDES * rows
     half = length // PAIR
     chips = owners // CORES
-    behind = max(chips // 4 - 1, 0)
+    side_chips = chips // SIDES
+    pairs = exp_dev // PAIR
+    behind = max(side_chips // 2 - 1, 0)
     me = lax.axis_index("expert")
     here = lax.axis_index("hidden")
+    chip, core = me // CORES, lax.rem(me, CORES)
     x, y = here // RING, lax.rem(here, RING)
 
     def hidden_at(dx, dy):
@@ -86,20 +90,31 @@
     def neighbour(part, axis, step):
         return (me, place(part, step, 0) if axis == 0 else place(part, 0, step))
 
+    barrier = pltpu.get_barrier_semaphore()
+
+    def greet(i, carry):
+        offset = owners // 2 + jnp.where(lax.rem(i, 2) == 1, (i + 1) // 2, -((i + 1) // 2))
+        pl.semaphore_signal(barrier, inc=1, device_id=(lax.rem(me + offset, owners), here), device_id_type=MESH)
+        return carry
+
+    lax.fori_loop(0, owners - 1, greet, 0)
+    inputs = [
+        pltpu.make_async_copy(src, dst, in_sem.at[number])
+        for number, (src, dst) in enumerate(
+            ((routes_hbm, routes_ref), (tokens_hbm, tokens_ref), (cot_hbm, cot_ref), (gate_hbm, gate_ref))
+        )
+    ]
+    for copy in inputs:
+        copy.start()
+    for step in (1, -1, 2):
+        for axis in (0, 1):
+            pl.semaphore_signal(barrier, inc=1, device_id=neighbour(0, axis, step), device_id_type=MESH)
     wint_copy = pltpu.make_async_copy(wint_ref, wint_v, w_sem.at[0])
     wout_copy = pltpu.make_async_copy(wout_ref, wout_v, w_sem.at[1])
     wint_copy.start()
     wout_copy.start()
-    barrier = pltpu.get_barrier_semaphore()
-
-    def greet(i, carry):
-        pl.semaphore_signal(barrier, inc=1, device_id=(lax.rem(me + i, owners), here), device_id_type=MESH)
-        return carry
-
-    lax.fori_loop(1, owners, greet, 0)
-    for step in (1, -1, 2):
-        for axis in (0, 1):
-            pl.semaphore_signal(barrier, inc=1, device_id=neighbour(0, axis, step), device_id_type=MESH)
+    for copy in inputs:
+        copy.wait()
 
     routes = routes_ref[...]
     experts = owners * exp_dev
@@ -109,7 +124,11 @@
     ).astype(BF16)
     before = dot(matches.astype(BF16), earlier)
     slot = jnp.sum(before * matches, axis=0, keepdims=True).astype(jnp.int32)
-    pos = routes * CAP + slot
+    owner = routes // exp_dev
+    pair_at = (routes & (exp_dev - 1)) // PAIR
+    number_at = (chip - owner // CORES + behind + chips) & (chips - 1)
+    block_at = ((number_at // side_chips * pairs + pair_at) * side_chips + (number_at & (side_chips - 1))) * CORES
+    pos = (block_at + (owner & (CORES - 1))) * rows + (routes & (PAIR - 1)) * CAP + slot
     scaled = gate_ref[...] * cot_ref[...].astype(F32)
     empty = jnp.zeros((LANES - 2 * feat, tok), BF16)
     both = jnp.concatenate([tokens_ref[...], scaled.astype(BF16), empty], axis=0)
@@ -120,15 +139,11 @@
 
     pl.semaphore_wait(barrier, owners - 1 + 6)
 
-    chip, core = me // CORES, lax.rem(me, CORES)
-    side_chips = chips // SIDES
-    pairs = exp_dev // PAIR
-
     def block(number):
         return pl.ds(pl.multiple_of(number * rows, rows), rows)
 
     def exchange(c, outward, src, dst, send_sem, recv_sem):
-        side, pair = c // pairs, c % pairs
+        side = c // pairs
         for number in sorted(
             range(side_chips), key=lambda k: -min((side * side_chips + k - behind) % chips, (behind - side * side_chips - k) % chips)
         ):
@@ -137,10 +152,8 @@
             for other in range(CORES):
                 to_core = lax.rem(core + other, CORES)
                 to = lax.rem(chip + way + chips, chips) * CORES + to_core
-                if outward:
-                    take, put = to * pairs + pair, (c * side_chips + number) * CORES + core
-                else:
-                    take, put = (c * side_chips + number) * CORES + to_core, me * pairs + pair
+                take = (c * side_chips + number) * CORES + to_core
+                put = (c * side_chips + number) * CORES + core
                 if ahead == 0 and other == 0:
                     dst[block(put), :] = src[block(take), :]
                 else:
@@ -307,10 +320,12 @@
     for e in range(exp_dev):
         weight_grads(e)
 
-    for p in range(CHUNKS):
+    taken = jnp.zeros((LANES, tok), F32)
+    for p in BACK:
         exchange_wait(p, back_v, back_recv)
-    turned = jnp.transpose(back_v[...].astype(F32)).astype(BF16)
-    taken = dot(turned, chosen_v[...])
+        at = slice(p * length, (p + 1) * length)
+        turned = jnp.transpose(back_v[at].astype(F32)).astype(BF16)
+        taken = taken + dot(turned, chosen_v[at])
     layer_ref[...] = (gate_ref[...] * taken[0:feat]).astype(BF16)
     gtok_ref[...] = taken[feat:2 * feat].astype(BF16)
 
@@ -328,16 +343,22 @@
 
 def hand_over(*refs):
     count = (len(refs) - 2) // 3
-    given, outs, held = refs[:count], refs[count:2 * count], refs[2 * count:3 * count]
     in_sem, out_sem = refs[3 * count:]
-    into = [pltpu.make_async_copy(given[i], held[i], in_sem.at[i]) for i in range(count)]
-    out = [pltpu.make_async_copy(held[i], outs[i], out_sem.at[i]) for i in range(count)]
+    pieces = []
+    for i in range(count):
+        three = [refs[i + k * count] for k in range(3)]
+        if len(three[0].shape) == 3:
+            pieces += [[ref.at[e] for ref in three] for e in range(three[0].shape[0])]
+        else:
+            pieces.append(three)
+    into = [pltpu.make_async_copy(given, held, in_sem.at[i]) for i, (given, out, held) in enumerate(pieces)]
+    away = [pltpu.make_async_copy(held, out, out_sem.at[i]) for i, (given, out, held) in enumerate(pieces)]
     for copy in into:
         copy.start()
-    for i in range(count):
-        into[i].wait()
-        out[i].start()
-    for copy in out:
+    for first, second in zip(into, away):
+        first.wait()
+        second.start()
+    for copy in away:
         copy.wait()
 
 
@@ -363,9 +384,13 @@
             jax.ShapeDtypeStruct((exp_dev, units, width), BF16),
             jax.ShapeDtypeStruct((exp_dev, units, width), BF16),
         ),
-        in_specs=[vmem, vmem, vmem, hbm, hbm, vmem],
+        in_specs=[hbm] * 6,
         out_specs=(vmem, vmem, hbm, hbm),
         scratch_shapes=[
+            pltpu.VMEM((feat, tok), BF16),
+            pltpu.VMEM((1, tok), jnp.int32),
+            pltpu.VMEM((1, tok), F32),
+            pltpu.VMEM((feat, tok), BF16),
             pltpu.VMEM((slots, tok), BF16),
             rows, rows, rows, rows,
             pltpu.VMEM((2, CHUNKS, blocks, feat, length), BF16),
@@ -377,6 +402,7 @@
             pltpu.VMEM((exp_dev, units, slots // exp_dev), BF16),
             pltpu.VMEM((exp_dev, units, slots // exp_dev), BF16),
             weights, weights,
+            dma((4,)),
             dma((2,)),
             dma((2, exp_dev)),
             dma((CHUNKS,)),
@@ -400,7 +426,7 @@
         out_shape=tuple(jax.ShapeDtypeStruct(out.shape, out.dtype) for out in outs),
         in_specs=[hbm] * len(outs),
         out_specs=(hbm,) * len(outs),
-        scratch_shapes=[pltpu.VMEM(out.shape, out.dtype) for out in outs] + [dma((len(outs),)), dma((len(outs),))],
+        scratch_shapes=[pltpu.VMEM(out.shape, out.dtype) for out in outs] + [dma((2 + 2 * exp_dev,)), dma((2 + 2 * exp_dev,))],
         compiler_params=pltpu.CompilerParams(vmem_limit_bytes=60 * 1024 * 1024),
         name="hand_over",
     )(*outs)

time: 81.9 us -> 80.4 us (0.982)
  Pallas kernels: 81 us -> 79.6 us
    pallas_call x1, Pallas kernels: 78.2 us -> 77 us  [local(): pl.pallas_call(kernel, out_shape=(jax.ShapeDtypeStruct((feat, tok), BF16)...]
where the time goes in v3:
time: 80.4 us; the launch traced here: 80.2 us
  Pallas kernels  79.6 us (99%)
    pallas_call x1, Pallas kernels, local(): pl.pallas_call(kernel, out_shape=(jax.ShapeDtypeStruct((feat, tok), BF16)...  77 us
    pallas_call x1, Pallas kernels, local(): pl.pallas_call(hand_over, out_shape=tuple((jax.ShapeDtypeStruct(out.shape...  2.59 us

profile of v3, /device:TPU:1, one launch (start us, length us, event | category | flops | bytes accessed | tf_op | source)
XLA Modules:
  0.0 80.2 jit_solution(7065939617518585696)
XLA Ops:
  0.6 77.0 %expert_layer.1 = (bf16[48,512]{1,0:T(8,128)(2,1)}, bf16[48,512]{1,0:T(8,128)(2,1)}, bf16[4,192,768]{2,1,0:T(8,128)(2,1)}, bf16[4,192,768]{2,1,0:T(8,128)(2,1)}) custom-call(bf16[48,512]{1,0:T(8,128)(2,1)} %bitcast.9, s32[1,512]{1,0:T(1,128)} %bitcast.11, f32[1,512]{1,0:T(1,128)} %bitcast.12, bf16[4,192,768]{2,1,0:T(8,128)(2,1)} %bitcast.8, ...), custom_call_target="tpu_custom_call" | custom-call | tf_op jit(solution)/shard_map/expert_layer/pallas_call | solution.py:379
  77.6 2.6 %hand_over.1 = (bf16[48,512]{1,0:T(8,128)(2,1)}, bf16[48,512]{1,0:T(8,128)(2,1)}, bf16[4,192,768]{2,1,0:T(8,128)(2,1)}, bf16[4,192,768]{2,1,0:T(8,128)(2,1)}) custom-call(bf16[48,512]{1,0:T(8,128)(2,1)} %get-tuple-element.12.refs_0_, bf16[48,512]{1,0:T(8,128)(2,1)} %get-tuple-element.13.refs_1_, bf16[4,192,768]{2,1,0:T(8,128)(2,1)} %get-tuple-element.14.refs_2_, ...), custom_call_target="tpu_custom_call" | custom-call | tf_op jit(solution)/shard_map/hand_over/pallas_call | solution.py:424

commit v4 on v3

--- a/solution.py
+++ b/solution.py
@@ -28,15 +28,15 @@
 ITEM = {2: 0, 1: 1, -1: 2, 0: 3}
 
 ORDER = (
-    ("S", 0), ("S", 1), ("F", 0, -1), ("F", 0, 1), ("R", 0, 0), ("F", 0, 2), ("F", 1, -1), ("F", 1, 1),
-    ("S", 2), ("R", 1, 0), ("F", 1, 2), ("R", 0, -1), ("R", 0, 1), ("R", 0, 2), ("R", 1, -1), ("R", 1, 1),
-    ("F", 2, -1), ("S", 3), ("F", 2, 1), ("R", 2, 0), ("F", 2, 2), ("R", 1, 2), ("R", 2, -1), ("F", 3, -1),
-    ("F", 3, 1), ("R", 3, 0), ("F", 3, 2), ("R", 2, 1), ("R", 2, 2), ("C", 1, 0), ("C", 1, 1), ("R", 3, -1),
-    ("R", 3, 1), ("R", 3, 2), ("C", 2, 0), ("C", 2, 1), ("M", 1, 2), ("M", 1, 1), ("M", 1, -1), ("M", 1, 0),
-    ("C", 3, 0), ("C", 3, 1), ("M", 2, 2), ("M", 2, 1), ("M", 2, -1), ("M", 2, 0), ("U", 1, 2), ("U", 1, 1),
-    ("U", 1, -1), ("C", 0, 0), ("C", 0, 1), ("M", 3, 1), ("M", 3, -1), ("M", 3, 2), ("M", 3, 0), ("U", 2, 2),
-    ("U", 2, 1), ("U", 2, -1), ("Z", 1), ("M", 0, 2), ("M", 0, 1), ("M", 0, -1), ("M", 0, 0), ("U", 3, 1),
-    ("U", 3, -1), ("U", 3, 2), ("Z", 2), ("U", 0, 2), ("U", 0, 1), ("U", 0, -1), ("Z", 3), ("Z", 0),
+    ("S", 0), ("F", 0, -1), ("F", 0, 1), ("R", 0, 0), ("F", 0, 2), ("S", 2), ("R", 0, -1), ("R", 0, 1),
+    ("R", 0, 2), ("F", 2, -1), ("F", 2, 1), ("S", 3), ("R", 2, 0), ("F", 2, 2), ("S", 1), ("R", 2, -1),
+    ("R", 2, 1), ("F", 3, -1), ("F", 3, 1), ("R", 3, 0), ("F", 3, 2), ("R", 2, 2), ("F", 1, -1), ("F", 1, 1),
+    ("R", 1, 0), ("F", 1, 2), ("R", 3, -1), ("R", 3, 1), ("R", 3, 2), ("C", 2, 0), ("C", 2, 1), ("R", 1, -1),
+    ("R", 1, 1), ("R", 1, 2), ("C", 3, 0), ("C", 3, 1), ("M", 2, 2), ("M", 2, 1), ("M", 2, -1), ("M", 2, 0),
+    ("C", 1, 0), ("C", 1, 1), ("M", 3, 2), ("M", 3, 1), ("M", 3, -1), ("M", 3, 0), ("U", 2, 2), ("U", 2, 1),
+    ("U", 2, -1), ("C", 0, 0), ("C", 0, 1), ("M", 1, 2), ("M", 1, 1), ("M", 1, -1), ("M", 1, 0), ("U", 3, 2),
+    ("U", 3, 1), ("U", 3, -1), ("Z", 2), ("M", 0, 2), ("M", 0, 1), ("M", 0, -1), ("M", 0, 0), ("U", 1, 2),
+    ("U", 1, 1), ("U", 1, -1), ("Z", 3), ("U", 0, 2), ("U", 0, 1), ("U", 0, -1), ("Z", 1), ("Z", 0),
 )
 BACK = [_step[1] for _step in ORDER if _step[0] == "Z"]
 
@@ -201,7 +201,7 @@
             turned = jnp.transpose(arrived[:, e].reshape(half, LANES))
             for part in range(2):
                 xg_v[part, p, here, :, e * half:(e + 1) * half] = turned[part * feat:(part + 1) * feat].astype(BF16)
-        for axis, step in ((0, 1), (0, -1), (0, 2), (1, 1), (1, -1)):
+        for axis, step in ((0, 2), (0, 1), (0, -1), (1, 1), (1, -1)):
             for part in range(2):
                 ag_send_to(part, p, 0, 0, None, axis, step)
 

time: 80.4 us -> 81.7 us (1.016)
  Pallas kernels: 79.6 us -> 80.9 us
    pallas_call x1, Pallas kernels: 77 us -> 78.3 us  [local(): pl.pallas_call(kernel, out_shape=(jax.ShapeDtypeStruct((feat, tok), BF16)...]
where the time goes in v4:
time: 81.7 us; the launch traced here: 81.5 us
  Pallas kernels  80.9 us (99%)
    pallas_call x1, Pallas kernels, local(): pl.pallas_call(kernel, out_shape=(jax.ShapeDtypeStruct((feat, tok), BF16)...  78.3 us
    pallas_call x1, Pallas kernels, local(): pl.pallas_call(hand_over, out_shape=tuple((jax.ShapeDtypeStruct(out.shape...  2.59 us

profile of v4, /device:TPU:1, one launch (start us, length us, event | category | flops | bytes accessed | tf_op | source)
XLA Modules:
  0.0 81.5 jit_solution(5232528880688195363)
XLA Ops:
  0.6 78.3 %expert_layer.1 = (bf16[48,512]{1,0:T(8,128)(2,1)}, bf16[48,512]{1,0:T(8,128)(2,1)}, bf16[4,192,768]{2,1,0:T(8,128)(2,1)}, bf16[4,192,768]{2,1,0:T(8,128)(2,1)}) custom-call(bf16[48,512]{1,0:T(8,128)(2,1)} %bitcast.9, s32[1,512]{1,0:T(1,128)} %bitcast.11, f32[1,512]{1,0:T(1,128)} %bitcast.12, bf16[4,192,768]{2,1,0:T(8,128)(2,1)} %bitcast.8, ...), custom_call_target="tpu_custom_call" | custom-call | tf_op jit(solution)/shard_map/expert_layer/pallas_call | solution.py:379
  78.9 2.6 %hand_over.1 = (bf16[48,512]{1,0:T(8,128)(2,1)}, bf16[48,512]{1,0:T(8,128)(2,1)}, bf16[4,192,768]{2,1,0:T(8,128)(2,1)}, bf16[4,192,768]{2,1,0:T(8,128)(2,1)}) custom-call(bf16[48,512]{1,0:T(8,128)(2,1)} %get-tuple-element.12.refs_0_, bf16[48,512]{1,0:T(8,128)(2,1)} %get-tuple-element.13.refs_1_, bf16[4,192,768]{2,1,0:T(8,128)(2,1)} %get-tuple-element.14.refs_2_, ...), custom_call_target="tpu_custom_call" | custom-call | tf_op jit(solution)/shard_map/hand_over/pallas_call | solution.py:424
